TPU v7x, 32 devices: a whole 2x2x4 slice. The times are simulated.
32 devices in a mesh: blk: 8 (over z, y), gy: 4 (over x, core).
Axes of the slice: x: 2, y: 2, z: 4, core: 2. Of those that a mesh axis runs over, the one named last changes fastest.
Arguments:
- image: float32 [1, 2048, 2048], P(None, 'blk', 'gy'), may hold values from -6 to 6
- measured: float32 [1, 16, 2816], P(None, 'blk'), may hold values from -6 to 6
- row_weight: float32 [16, 2816], P('blk'), may hold values from 0.25 to 2
- col_weight: float32 [2048, 2048], P('blk', 'gy'), may hold values from 1 to 8
- band_weight: bfloat16 [16, 2048, 128], P('blk', 'gy'), may hold values from -0.01171875 to 0.01171875
- band_shift: int32 [16, 8], replicated, may hold values from 0 to 3
Outputs:
- updated: float32 [1, 2048, 2048], P(None, 'blk', 'gy')
Inputs may be any that keep to these rules, and one draw needn't show every extreme that they name: band_shift[t, s] is the number of panels by which slab s's footprint under tilt t starts beyond panel s * 2.
All inputs are finite; a program needn't handle non-finite values.
Results may differ from a plain program's by a relative error of at most 0.0025.
Values may be sent and summed in bfloat16 or wider, within the bound.
A program may use at most 64 MiB of HBM per device.

v0:
```python
import math

import jax
import jax.numpy as jnp
from jax import lax
from jax.sharding import PartitionSpec as P

PW = 128


SMOOTH = 0.25


def with_halo(cells, sides, width):
    for axis, dim in sides:
        count = lax.axis_size(axis)
        ends = count - 1
        head = lax.slice_in_dim(cells, 0, width, axis=dim)
        tail = lax.slice_in_dim(cells, cells.shape[dim] - width, cells.shape[dim], axis=dim)
        cells = jnp.concatenate(
            [
                lax.ppermute(tail, axis, [(i, (i + 1) % count) for i in range(ends)]),
                cells,
                lax.ppermute(head, axis, [((i + 1) % count, i) for i in range(ends)]),
            ],
            axis=dim,
        )
    return cells


def shift_rows(rows, direction):
    col_count = rows.shape[-2]
    bit_count = (col_count - 1).bit_length()
    column_index = jnp.arange(col_count, dtype=jnp.int32)[:, None]
    for level in range(bit_count):
        moved = jnp.roll(rows, direction * (1 << level), axis=-1)
        chosen = column_index >> level & 1 == 1
        rows = jnp.where(chosen, moved, rows)
    return rows


def diagonal_sum(product):
    leading = product.shape[:-2]
    col_count, band_width = product.shape[-2:]
    keep_pads = [(0, 0)] * (len(leading) + 1)
    padded = jnp.pad(product, keep_pads + [(0, col_count)])
    return jnp.sum(shift_rows(padded, 1), axis=-2)


def band_rows(panels, col_count, band_width):
    leading = panels.shape[:-1]
    window_len = panels.shape[-1]
    repeated = jnp.broadcast_to(panels[..., None, :], leading + (col_count, window_len))
    return shift_rows(repeated, -1)[..., :band_width]


def per_device(image, measured, row_weight, col_weight, band_weight, band_shift):
    row_count, col_count, depth_count = image.shape
    local_tilts = measured.shape[1]
    detector_len = measured.shape[2]
    band_width = band_weight.shape[2]
    window_len = col_count + band_width
    block_count = lax.axis_size("blk")
    myself = lax.axis_index("blk")
    tilt_count = local_tilts * block_count
    per_slab = col_count // PW
    zero_index = jnp.int32(0)
    copies = image.astype(jnp.bfloat16)
    slab_bins = ((jnp.arange(block_count, dtype=jnp.int32) * per_slab)[None, :] + band_shift) * PW
    first_tilt = myself * local_tilts
    own_bins = lax.dynamic_slice_in_dim(slab_bins, first_tilt, local_tilts, 0)
    group_size = math.gcd(tilt_count, 8)
    all_weights = lax.all_gather(band_weight, "blk", axis=0, tiled=True)
    weight_groups = all_weights.reshape(
        tilt_count // group_size, group_size, depth_count, band_width
    )

    def place_windows(running, windows, source):
        for tilt_slot in range(local_tilts):
            offset = own_bins[tilt_slot, source]
            corner = (zero_index, jnp.int32(tilt_slot), offset)
            current = lax.dynamic_slice(running, corner, (row_count, 1, window_len))
            running = lax.dynamic_update_slice(
                running, current + windows[tilt_slot][:, None, :], corner
            )
        return running

    initial = jnp.zeros((row_count, local_tilts, detector_len), jnp.float32)

    def project_group(weights):
        product = jnp.einsum("yiz,tzd->tyid", copies, weights, preferred_element_type=jnp.float32)
        return diagonal_sum(product)

    windows = lax.map(project_group, weight_groups)
    windows = windows.reshape(block_count, local_tilts, row_count, window_len)
    received = lax.all_to_all(windows, "blk", split_axis=0, concat_axis=0, tiled=True)

    def add_source(source, running):
        return place_windows(
            running, lax.dynamic_index_in_dim(received, source, 0, keepdims=False), source
        )

    partial_sum = lax.fori_loop(0, block_count, add_source, initial)
    projection = lax.psum(partial_sum, "gy")
    weighted = (row_weight[None] * (measured - projection)).astype(jnp.bfloat16)

    def cut_panels(slab_offsets):
        pieces = [
            lax.dynamic_slice(
                weighted[:, tilt_slot],
                (zero_index, slab_offsets[tilt_slot]),
                (row_count, window_len),
            )
            for tilt_slot in range(local_tilts)
        ]
        return jnp.stack(pieces, axis=1)

    outgoing = jax.vmap(cut_panels, in_axes=1, out_axes=1)(own_bins)
    arrived = lax.all_to_all(outgoing, "blk", split_axis=1, concat_axis=1, tiled=True)
    panels = arrived.reshape(row_count, tilt_count, window_len)
    panel_groups = panels.reshape(
        row_count, tilt_count // group_size, group_size, window_len
    ).transpose(1, 0, 2, 3)

    def back_group(running, operands):
        panel_part, weight_part = operands
        sheared = band_rows(panel_part, col_count, band_width)
        added = jnp.einsum(
            "ytid,tzd->yiz", sheared, weight_part, preferred_element_type=jnp.float32
        )
        return (running + added, None)

    start_back = jnp.zeros((row_count, col_count, depth_count), jnp.float32)
    backed, leftover = lax.scan(back_group, start_back, (panel_groups, weight_groups))
    padded_depth = with_halo(image.astype(jnp.bfloat16), (("gy", 2),), 1).astype(image.dtype)
    return (
        image
        + col_weight[None] * backed
        + SMOOTH * (padded_depth[:, :, :-2] + padded_depth[:, :, 2:] - 2.0 * image)
    )


def solution(mesh):
    return jax.shard_map(
        per_device,
        mesh=mesh,
        in_specs=(
            P(None, "blk", "gy"),
            P(None, "blk", None),
            P("blk", None),
            P("blk", "gy"),
            P("blk", "gy", None),
            P(),
        ),
        out_specs=P(None, "blk", "gy"),
        check_vma=False,
    )
```

profile of v0, /device:TPU:0, one launch (start us, length us, event | category | flops | bytes accessed | tf_op | source)
XLA Modules:
  0.0 203.8 jit_solution(14922307778124006677)
XLA Ops:
  7.3 1.1 convert_element_type.22
  9.0 3.0 %collective-permute-start = (bf16[1,256,1]{2,1,0:T(8,128)(2,1)}, bf16[1,256,1]{2,1,0:T(8,128)(2,1)}, u32[]{:S(2)}, u32[]{:S(2)}) collective-permute-start(bf16[1,256,1]{2,1,0:T(8,128)(2,1)} %get-tuple-element.283), channel_id=1, source_target_pairs={{0,1},{1,2},{2,3},{4,5},{5,6},{6,7},{8,9},{9,10},{10,11},{12,13},{... | collective-permute-start | bytes 1544 | tf_op jit(solution)/shard_map/ppermute | solution.py:22
  12.0 1.3 collective-permute-start.1
  15.5 46.0 %all-gather.2.cloned.1.call-done = bf16[16,512,128]{2,1,0:T(8,128)(2,1)} async-done(((bf16[2,512,128]{2,1,0:T(8,128)(2,1)}), bf16[16,512,128]{2,1,0:T(8,128)(2,1)}) %all-gather.2.cloned.1.call-update) | async-done | bytes 2097168 | tf_op jit(solution)/shard_map/all_gather | solution.py:73
  61.5 14.9 %while.38 = (s32[]{:T(128)}, f32[2,8,1,384]{3,2,1,0:T(1,128)}, bf16[2,8,512,128]{3,2,1,0:T(8,128)(2,1)}, bf16[1,256,512]{2,1,0:T(8,128)(2,1)S(1)}, s32[]{:T(128)}) while((s32[]{:T(128)}, f32[2,8,1,384]{3,2,1,0:T(1,128)}, bf16[2,8,512,128]{3,2,1,0:T(8,128)(2,1)}, bf16[1,256,512]{2,1,0:T(8,128)(2,1)S(1)}, s32[]{:T(128)}) %tuple.126), condition=%wide.region_2.3_spmd, body=%wide.region_0.2_spmd.sunk | while | flops 281021440 | bytes 108389440 | solution.py:94
  61.5 1.7 convolution_bitcast_fusion.3
  69.0 1.7 convolution_bitcast_fusion.3
  76.4 3.3 %all-to-all-start = ((f32[8,2,1,384]{3,2,1,0:T(1,128)}), f32[8,2,1,384]{3,2,1,0:T(1,128)S(1)}, u32[]{:S(2)}, u32[]{:S(2)}) async-start(f32[8,2,1,384]{3,2,1,0:T(1,128)} %bitcast.12), calls=%async_computation | async-start | bytes 49152 | tf_op jit(solution)/shard_map/all_to_all | solution.py:96
  79.9 6.4 %all-to-all-done = f32[8,2,1,384]{3,2,1,0:T(1,128)S(1)} async-done(((f32[8,2,1,384]{3,2,1,0:T(1,128)}), f32[8,2,1,384]{3,2,1,0:T(1,128)S(1)}, u32[]{:S(2)}, u32[]{:S(2)}) %all-to-all-start) | async-done | bytes 24608 | tf_op jit(solution)/shard_map/all_to_all | solution.py:96
  86.3 35.3 %while.39 = (s32[]{:T(128)}, f32[1,2,2816]{2,1,0:T(2,128)S(1)}, s32[2,8]{1,0:T(2,128)S(1)}, f32[8,2,1,384]{3,2,1,0:T(1,128)S(1)}, s32[]{:T(128)}, /*index=5*/s32[]{:T(128)}, s32[]{:T(128)}, s32[]{}) while((s32[]{:T(128)}, f32[1,2,2816]{2,1,0:T(2,128)S(1)}, s32[2,8]{1,0:T(2,128)S(1)}, f32[8,2,1,384]{3,2,1,0:T(1,128)S(1)}, s32[]{:T(128)}, ...), condition=%wide.region_4.5_spmd, body=%wide.region_3.4_spmd.sunk | while | flops 777 | bytes 15573 | solution.py:103
  121.7 10.3 %psum.7 = f32[1,2,2816]{2,1,0:T(2,128)S(1)} all-reduce(f32[1,2,2816]{2,1,0:T(2,128)S(1)} %get-tuple-element.160), channel_id=1, replica_groups=mesh['blk'=8,'gy'=4] {'gy'}, use_global_device_ids=true, to_apply=%region_5.6 | all-reduce | flops 5632 | bytes 45056 | tf_op jit(solution)/shard_map/psum | solution.py:104
  132.0 11.8 %while.40 = (s32[]{:T(128)}, bf16[1,2816]{1,0:T(2,128)(2,1)S(1)}, s32[8,2]{0,1:T(2,128)S(1)}, bf16[8,1,384]{2,0,1:T(8,128)(2,1)S(1)}, s32[]{:T(128)}, /*index=5*/s32[]{:T(128)}) while((s32[]{:T(128)}, bf16[1,2816]{1,0:T(2,128)(2,1)S(1)}, s32[8,2]{0,1:T(2,128)S(1)}, bf16[8,1,384]{2,0,1:T(8,128)(2,1)S(1)}, s32[]{:T(128)}, /*index=5*/s32[]{:T(128)}) %tuple.118), condition=%wide.while_cond, body=%wide.while_body.sunk | while | flops 2 | bytes 3177 | solution.py:109
  132.7 0.8 dynamic-slice_bitcast_fusion.6
  134.2 0.8 dynamic-slice_bitcast_fusion.6
  135.7 0.8 dynamic-slice_bitcast_fusion.6
  137.2 0.8 dynamic-slice_bitcast_fusion.6
  138.6 0.8 dynamic-slice_bitcast_fusion.6
  140.1 0.8 dynamic-slice_bitcast_fusion.6
  141.6 0.8 dynamic-slice_bitcast_fusion.6
  143.1 0.8 dynamic-slice_bitcast_fusion.6
  143.9 10.7 %while.41 = (s32[]{:T(128)}, bf16[1,2816]{1,0:T(2,128)(2,1)S(1)}, s32[8,2]{0,1:T(2,128)S(1)}, bf16[8,1,384]{2,0,1:T(8,128)(2,1)S(1)}, s32[]{:T(128)}, /*index=5*/s32[]{:T(128)}) while((s32[]{:T(128)}, bf16[1,2816]{1,0:T(2,128)(2,1)S(1)}, s32[8,2]{0,1:T(2,128)S(1)}, bf16[8,1,384]{2,0,1:T(8,128)(2,1)S(1)}, s32[]{:T(128)}, /*index=5*/s32[]{:T(128)}) %tuple.115), condition=%wide.while_cond.1, body=%wide.while_body.1.sunk | while | flops 2 | bytes 3177 | solution.py:109
  155.2 3.5 %all-to-all-start.1 = ((bf16[1,8,2,384]{3,2,0,1:T(2,128)(2,1)}), bf16[1,8,2,384]{3,2,0,1:T(2,128)(2,1)S(1)}, u32[]{:S(2)}, u32[]{:S(2)}) async-start(bf16[1,8,2,384]{3,2,0,1:T(2,128)(2,1)} %copy.33), calls=%async_computation.1 | async-start | bytes 24576 | tf_op jit(solution)/shard_map/all_to_all | solution.py:119
  158.7 1.9 maximum_convert_fusion
  160.6 4.4 %all-to-all-done.1 = bf16[1,8,2,384]{3,2,0,1:T(2,128)(2,1)S(1)} async-done(((bf16[1,8,2,384]{3,2,0,1:T(2,128)(2,1)}), bf16[1,8,2,384]{3,2,0,1:T(2,128)(2,1)S(1)}, u32[]{:S(2)}, u32[]{:S(2)}) %all-to-all-start.1) | async-done | bytes 12320 | tf_op jit(solution)/shard_map/all_to_all | solution.py:119
  165.0 29.1 %while.42 = (s32[]{:T(128)}, f32[1,256,512]{2,1,0:T(8,128)}, bf16[2,1,8,384]{3,2,0,1:T(8,128)(2,1)S(1)}, bf16[2,8,512,128]{3,2,1,0:T(8,128)(2,1)}, s32[]{:T(128)}, /*index=5*/s32[]{:T(128)}) while((s32[]{:T(128)}, f32[1,256,512]{2,1,0:T(8,128)}, bf16[2,1,8,384]{3,2,0,1:T(8,128)(2,1)S(1)}, bf16[2,8,512,128]{3,2,1,0:T(8,128)(2,1)}, ...), condition=%wide.region_7.8_spmd.clone, body=%wide.region_6.7_spmd.clone.sunk | while | flops 301471744 | bytes 67193432 | solution.py:134
  167.1 1.1 maximum_select_fusion.34
  176.3 0.9 slice.383
  177.2 2.3 %fusion.41 = f32[1,256,512]{2,1,0:T(8,128)} fusion(bf16[2,8,512,128]{3,2,1,0:T(8,128)(2,1)S(1)} %copy-done, s32[]{:T(128)} %get-tuple-element.503, bf16[1,8,256,128]{3,2,1,0:T(8,128)(2,1)} %slice.383, bf16[1,8,256,256]{3,2,1,0:T(8,128)(2,1)S(1)} %slice.384, f32[1,256,512]{2,1,0:T(8,128)} %get-tuple-element.504, ...), kind=kOutput, calls=%fused_computation.42.clone.1 | convolution fusion | flops 270008320 | bytes 3670533 | tf_op jit(solution)/shard_map/while/body/eval_jaxpr/ytid,tzd->yiz/dot_general | solution.py:128
  181.6 1.1 maximum_select_fusion.34
  190.8 0.9 slice.383
  191.7 2.5 %fusion.41 = f32[1,256,512]{2,1,0:T(8,128)} fusion(bf16[2,8,512,128]{3,2,1,0:T(8,128)(2,1)S(1)} %copy-done, s32[]{:T(128)} %get-tuple-element.503, bf16[1,8,256,128]{3,2,1,0:T(8,128)(2,1)} %slice.383, bf16[1,8,256,256]{3,2,1,0:T(8,128)(2,1)S(1)} %slice.384, f32[1,256,512]{2,1,0:T(8,128)} %get-tuple-element.504, ...), kind=kOutput, calls=%fused_computation.42.clone.1 | convolution fusion | flops 270008320 | bytes 3670533 | tf_op jit(solution)/shard_map/while/body/eval_jaxpr/ytid,tzd->yiz/dot_general | solution.py:128
  194.2 2.8 %fusion.19 = f32[1,256,512]{2,1,0:T(8,128)} fusion(f32[1,256,514]{2,1,0:T(8,128)} %maximum_convert_fusion, f32[1,256,512]{2,1,0:T(8,128)} %param.12, f32[1,256,512]{2,1,0:T(8,128)} %get-tuple-element.161, f32[256,512]{1,0:T(8,128)} %param.15), kind=kLoop, calls=%fused_computation.65 | loop fusion | flops 917504 | bytes 3145728 | tf_op jit(solution)/shard_map/add | solution.py:137
  (263 shorter events, 59.6 us)
Async XLA Ops:
  6.5 55.0 %all-gather.2.cloned.1.call-start = ((), (), s32[]{:S(2)}) async-start(), calls=%async_computation.2 | async-start | bytes 2359296 | tf_op jit(solution)/shard_map/all_gather | solution.py:73
  9.0 149.7 %collective-permute-start = (bf16[1,256,1]{2,1,0:T(8,128)(2,1)}, bf16[1,256,1]{2,1,0:T(8,128)(2,1)}, u32[]{:S(2)}, u32[]{:S(2)}) collective-permute-start(bf16[1,256,1]{2,1,0:T(8,128)(2,1)} %get-tuple-element.283), channel_id=1, source_target_pairs={{0,1},{1,2},{2,3},{4,5},{5,6},{6,7},{8,9},{9,10},{10,11},{12,13},{... | collective-permute-start | bytes 1544 | tf_op jit(solution)/shard_map/ppermute | solution.py:22
  12.0 146.7 %collective-permute-start.1 = (bf16[1,256,1]{2,1,0:T(8,128)(2,1)}, bf16[1,256,1]{2,1,0:T(8,128)(2,1)}, u32[]{:S(2)}, u32[]{:S(2)}) collective-permute-start(bf16[1,256,1]{2,1,0:T(8,128)(2,1)} %get-tuple-element.284), channel_id=1, source_target_pairs={{1,0},{2,1},{3,2},{5,4},{6,5},{7,6},{9,8},{10,9},{11,10},{13,12},{... | collective-permute-start | bytes 1544 | tf_op jit(solution)/shard_map/ppermute | solution.py:24
  14.2 0.6 copy-start.1
  61.5 18.3 %copy-start.5 = (s32[8]{0:T(128)S(1)}, s32[8]{0:T(128)}, u32[]{:S(2)}) copy-start(s32[8]{0:T(128)} %get-tuple-element.237) | copy-start | bytes 100
  61.5 18.3 %copy-start.6 = (s32[8]{0:T(128)S(1)}, s32[8]{0:T(128)}, u32[]{:S(2)}) copy-start(s32[8]{0:T(128)} %get-tuple-element.238) | copy-start | bytes 100
  61.5 18.3 %copy-start.2 = (s32[2,8]{0,1:T(8,128)S(1)}, s32[2,8]{0,1:T(8,128)}, u32[]{:S(2)}) copy-start(s32[2,8]{0,1:T(8,128)} %copy-done.1) | copy-start | bytes 196
  61.5 70.4 %copy-start.3 = (f32[2,2816]{1,0:T(2,128)S(1)}, f32[2,2816]{1,0:T(2,128)}, u32[]{:S(2)}) copy-start(f32[2,2816]{1,0:T(2,128)} %param.14) | copy-start | bytes 67588
  61.5 70.4 %copy-start.4 = (f32[1,2,2816]{2,1,0:T(2,128)S(1)}, f32[1,2,2816]{2,1,0:T(2,128)}, u32[]{:S(2)}) copy-start(f32[1,2,2816]{2,1,0:T(2,128)} %param.13) | copy-start | bytes 67588
  76.4 9.9 %all-to-all-start = ((f32[8,2,1,384]{3,2,1,0:T(1,128)}), f32[8,2,1,384]{3,2,1,0:T(1,128)S(1)}, u32[]{:S(2)}, u32[]{:S(2)}) async-start(f32[8,2,1,384]{3,2,1,0:T(1,128)} %bitcast.12), calls=%async_computation | async-start | bytes 49152 | tf_op jit(solution)/shard_map/all_to_all | solution.py:96
  155.2 9.8 %all-to-all-start.1 = ((bf16[1,8,2,384]{3,2,0,1:T(2,128)(2,1)}), bf16[1,8,2,384]{3,2,0,1:T(2,128)(2,1)S(1)}, u32[]{:S(2)}, u32[]{:S(2)}) async-start(bf16[1,8,2,384]{3,2,0,1:T(2,128)(2,1)} %copy.33), calls=%async_computation.1 | async-start | bytes 24576 | tf_op jit(solution)/shard_map/all_to_all | solution.py:119
  175.5 1.7 copy-start
  190.0 1.7 copy-start
Sparse Core Ops, SparseCore 0:
  9.5 51.9 all-gather.1
where the time goes:
time: 205 us; the launch traced here: 204 us
  waiting for transfers between devices  57.6 us (28%)
  local copies, waits for them, and re-layouts  49.3 us (24%)
  loops' own time  28.2 us (14%)
  other arithmetic  25.6 us (12%)
  between operations  13.6 us (7%)
  starting transfers between devices  11.1 us (5%)
  blocking collectives  10.3 us (5%)
  matrix products  8.25 us (4%)
    all_gather x1, waiting for transfers between devices, per_device(): all_weights = lax.all_gather(band_weight, 'blk', axis=0, tiled=True)  46 us
    another operation x1, loops' own time, per_device(): partial_sum = lax.fori_loop(0, block_count, add_source, initial)  27.2 us
    gather x64, local copies, waits for them, and re-layouts  22.3 us
    select_n x28, other arithmetic, shift_rows(): rows = jnp.where(chosen, moved, rows)  16.4 us
    slice x60, local copies, waits for them, and re-layouts, shift_rows(): moved = jnp.roll(rows, direction * (1 << level), axis=-1)  15.1 us
    psum x1, blocking collectives, per_device(): projection = lax.psum(partial_sum, 'gy')  10.3 us
    all_to_all x1, waiting for transfers between devices, per_device(): lax.all_to_all(windows, 'blk', split_axis=0, concat_axis=0, tiled=True)  6.42 us
    dot_general x2, matrix products, back_group(): jnp.einsum('ytid,tzd->yiz', sheared, weight_part, preferred_element_type=...  4.81 us
  transfers between devices with their start and end apart: 5, of which 3 were waited for; matrix products, arithmetic and copies ran while one was open for 25% of the time, Pallas kernels for 0%

commit v1 on v0

v1 whole, which is shorter than its diff:
```python
import functools

import jax
import jax.numpy as jnp
from jax import lax
from jax.experimental import pallas as pl
from jax.experimental.pallas import tpu as pltpu
from jax.sharding import PartitionSpec as P

PW = 128
SMOOTH = 0.25
SHIFTS = 4
MESH = pl.DeviceIdType.MESH


def roll_lanes(rows, amount):
    return pltpu.roll(rows, amount % rows.shape[1], 1)


def diagonal_sum(product):
    parts = [product[c : c + PW] for c in range(0, product.shape[0], PW)]
    rows = jnp.concatenate(parts + [jnp.zeros((PW, PW), jnp.float32)], axis=1)
    half = PW // 2
    while half >= 8:
        rows = rows[:half] + roll_lanes(rows[half:], half)
        half //= 2
    sub = lax.broadcasted_iota(jnp.int32, rows.shape, 0)
    for level in (4, 2, 1):
        rows = jnp.where(sub & level != 0, roll_lanes(rows, level), rows)
    return jnp.sum(rows, axis=0, keepdims=True)


def band_rows(line, col_count):
    rows = jnp.broadcast_to(line, (8, line.shape[1]))
    sub = lax.broadcasted_iota(jnp.int32, rows.shape, 0)
    for level in (4, 2, 1):
        rows = jnp.where(sub & level != 0, roll_lanes(rows, -level), rows)
    while rows.shape[0] < PW:
        rows = jnp.concatenate([rows, roll_lanes(rows, -rows.shape[0])], axis=0)
    return jnp.concatenate([rows[:, c : c + PW] for c in range(0, col_count, PW)], axis=0)


def kernel(
    blocks, groups,
    image_ref, measured_ref, row_ref, col_ref, band_ref, shift_ref, out_ref,
    weights, copies, shift_rows, placed, footprints, partial, cut, panels, edge_out, edge_in,
    up_sem, down_sem, side_sem, weight_sem,
    foot_send, foot_recv, part_send, part_recv, cut_send, cut_recv, edge_send, edge_recv,
):
    blk, gy = lax.axis_index("blk"), lax.axis_index("gy")
    line = blocks // 2
    spot, side = blk // 2, blk % 2
    local_tilts, depth, band_width = band_ref.shape
    col_count = image_ref.shape[0]
    detector_len = measured_ref.shape[1]
    per_slab = col_count // PW
    window_panels = per_slab + 1
    reach = window_panels + SHIFTS - 1

    edge_in[...] = jnp.zeros_like(edge_in)
    barrier = pltpu.get_barrier_semaphore()

    def greet_blk(step, carry):
        peer = lax.rem(blk + step, blocks)
        pl.semaphore_signal(barrier, inc=1, device_id=(peer, gy), device_id_type=MESH)
        return carry

    def greet_gy(step, carry):
        peer = lax.rem(gy + step, groups)
        pl.semaphore_signal(barrier, inc=1, device_id=(blk, peer), device_id_type=MESH)
        return carry

    lax.fori_loop(1, blocks, greet_blk, 0)
    lax.fori_loop(1, groups, greet_gy, 0)
    pl.semaphore_wait(barrier, blocks + groups - 2)

    def send_weights(block, sems, to):
        return pltpu.make_async_remote_copy(
            src_ref=weights.at[block], dst_ref=weights.at[block],
            send_sem=sems.at[block], recv_sem=weight_sem.at[block],
            device_id=(to, gy), device_id_type=MESH,
        )

    def send_up(block):
        return send_weights(block, up_sem, lax.rem(blk + 2, blocks))

    def send_down(block):
        return send_weights(block, down_sem, lax.rem(blk + blocks - 2, blocks))

    def send_side(block):
        return send_weights(block, side_sem, blk + 1 - 2 * side)

    def send_foot(block):
        return pltpu.make_async_remote_copy(
            src_ref=placed.at[block], dst_ref=footprints.at[blk],
            send_sem=foot_send.at[block], recv_sem=foot_recv.at[blk],
            device_id=(block, gy), device_id_type=MESH,
        )

    def foot_from(block):
        return pltpu.make_async_remote_copy(
            src_ref=placed.at[block], dst_ref=footprints.at[block],
            send_sem=foot_send.at[block], recv_sem=foot_recv.at[block],
            device_id=(block, gy), device_id_type=MESH,
        )

    def edge_copy(which, to):
        return pltpu.make_async_remote_copy(
            src_ref=edge_out.at[which], dst_ref=edge_in.at[which, pl.ds(0, 8)],
            send_sem=edge_send.at[which], recv_sem=edge_recv.at[which],
            device_id=(blk, to), device_id_type=MESH,
        )

    def tail_copy():
        return edge_copy(0, lax.rem(gy + 1, groups))

    def head_copy():
        return edge_copy(1, lax.rem(gy + groups - 1, groups))

    weights[blk] = band_ref[...]

    @pl.when(spot < line - 1)
    def _():
        send_up(blk).start()

    @pl.when(spot > 0)
    def _():
        send_down(blk).start()

    send_side(blk).start()

    copies[...] = image_ref[...].astype(jnp.bfloat16)
    slab = lax.broadcasted_iota(jnp.int32, shift_ref.shape, 1)
    own_shift = jnp.sum(jnp.where(slab == blk, shift_ref[...], 0), axis=1, keepdims=True)
    shift_rows[...] = jnp.broadcast_to(own_shift, shift_rows.shape)

    edge_out[0] = image_ref[:, depth - PW :].T[PW - 8 :]
    edge_out[1] = image_ref[:, :PW].T[:8]

    @pl.when(gy < groups - 1)
    def _():
        tail_copy().start()

    @pl.when(gy > 0)
    def _():
        head_copy().start()

    def wide(block):
        return jnp.concatenate([weights[block, t] for t in range(local_tilts)], axis=1)

    def project(block):
        product = jnp.dot(copies[...], wide(block), preferred_element_type=jnp.float32)
        for t in range(local_tilts):
            window = diagonal_sum(product[:, t * band_width : (t + 1) * band_width])
            shift = shift_rows[pl.ds(block * local_tilts + t, 1), :]
            for panel in range(reach):
                total = jnp.zeros((1, PW), jnp.float32)
                for k in range(SHIFTS):
                    if 0 <= panel - k < window_panels:
                        piece = window[:, (panel - k) * PW : (panel - k + 1) * PW]
                        total = jnp.where(shift == k, piece, total)
                placed[block, pl.ds(t, 1), pl.ds(panel * PW, PW)] = total

        @pl.when(block != blk)
        def _():
            send_foot(block).start()

        @pl.when(block == blk)
        def _():
            footprints[blk] = placed[blk]

    def gather_step(step, carry):
        below, above = spot - step, spot + step

        @pl.when((step > 0) & (below >= 0))
        def _():
            block = below * 2 + side
            send_up(block).wait_recv()

            @pl.when(spot < line - 1)
            def _():
                send_up(block).start()

            send_side(block).start()

        @pl.when((step > 0) & (above < line))
        def _():
            block = above * 2 + side
            send_down(block).wait_recv()

            @pl.when(spot > 0)
            def _():
                send_down(block).start()

            send_side(block).start()

        def visit(turn, carry):
            other = turn // 2
            far = step - other
            place = jnp.where(turn % 2 == 0, spot - far, spot + far)
            inside = (far >= 0) & (place >= 0) & (place < line) & ((far > 0) | (turn % 2 == 0))
            block = place * 2 + jnp.where(other == 0, side, 1 - side)

            @pl.when(inside)
            def _():
                @pl.when(other == 1)
                def _():
                    send_side(block).wait_recv()

                project(block)

            return carry

        return lax.fori_loop(0, 4, visit, carry)

    lax.fori_loop(0, line + 1, gather_step, 0)

    def take_foot(step, carry):
        foot_from(lax.rem(blk + step, blocks)).wait_recv()
        return carry

    lax.fori_loop(1, blocks, take_foot, 0)

    partial[gy] = jnp.zeros((local_tilts, detector_len), jnp.float32)
    for source in range(blocks):
        bins = pl.ds(source * per_slab * PW, reach * PW)
        partial[gy, :, bins] = partial[gy, :, bins] + footprints[source]

    def part_copy(to, slot):
        return pltpu.make_async_remote_copy(
            src_ref=partial.at[gy], dst_ref=partial.at[slot],
            send_sem=part_send.at[to], recv_sem=part_recv.at[slot],
            device_id=(blk, to), device_id_type=MESH,
        )

    def give_part(step, carry):
        part_copy(lax.rem(gy + step, groups), gy).start()
        return carry

    def take_part(step, carry):
        peer = lax.rem(gy + step, groups)
        part_copy(peer, peer).wait_recv()
        return carry

    lax.fori_loop(1, groups, give_part, 0)
    lax.fori_loop(1, groups, take_part, 0)

    projection = partial[0]
    for group in range(1, groups):
        projection = projection + partial[group]
    weighted = (row_ref[...] * (measured_ref[...] - projection)).astype(jnp.bfloat16)
    weighted = weighted.astype(jnp.float32)
    for block in range(blocks):
        start = block * per_slab * PW
        cut[block] = weighted[:, start : start + reach * PW]

    def cut_copy(to, slot):
        return pltpu.make_async_remote_copy(
            src_ref=cut.at[to], dst_ref=panels.at[slot],
            send_sem=cut_send.at[to], recv_sem=cut_recv.at[slot],
            device_id=(to, gy), device_id_type=MESH,
        )

    def give_cut(step, carry):
        cut_copy(lax.rem(blk + step, blocks), blk).start()
        return carry

    lax.fori_loop(1, blocks, give_cut, 0)
    panels[blk] = cut[blk]
    out_ref[...] = jnp.zeros_like(out_ref)

    def back_step(step, carry):
        source = lax.rem(blk + step, blocks)

        @pl.when(step > 0)
        def _():
            cut_copy(source, source).wait_recv()

        sheared = []
        for t in range(local_tilts):
            shift = shift_rows[pl.ds(source * local_tilts + t, 1), :]
            pieces = []
            for panel in range(window_panels):
                piece = panels[source, pl.ds(t, 1), pl.ds(panel * PW, PW)]
                for k in range(1, SHIFTS):
                    moved = panels[source, pl.ds(t, 1), pl.ds((panel + k) * PW, PW)]
                    piece = jnp.where(shift == k, moved, piece)
                pieces.append(piece)
            sheared.append(band_rows(jnp.concatenate(pieces, axis=1), col_count))
        rows = jnp.concatenate(sheared, axis=1).astype(jnp.bfloat16)
        out_ref[...] += lax.dot_general(
            rows, wide(source), (((1,), (1,)), ((), ())), preferred_element_type=jnp.float32
        )
        return carry

    lax.fori_loop(0, blocks, back_step, 0)

    @pl.when(gy > 0)
    def _():
        tail_copy().wait_recv()

    @pl.when(gy < groups - 1)
    def _():
        head_copy().wait_recv()

    before = edge_in[0].T[:, 7:8]
    after = edge_in[1].T[:, 0:1]
    chunk = 32
    lane = lax.broadcasted_iota(jnp.int32, (chunk, depth), 1)
    for top in range(0, col_count, chunk):
        rows = slice(top, top + chunk)
        here = image_ref[rows, :]
        left = jnp.where(lane == 0, before[rows], roll_lanes(here, 1))
        right = jnp.where(lane == depth - 1, after[rows], roll_lanes(here, -1))
        out_ref[rows, :] = (
            here + col_ref[rows, :] * out_ref[rows, :] + SMOOTH * (left + right - 2.0 * here)
        )

    @pl.when(gy < groups - 1)
    def _():
        tail_copy().wait_send()

    @pl.when(gy > 0)
    def _():
        head_copy().wait_send()

    def settle_line(place, carry):
        block = place * 2 + side

        @pl.when((place <= spot) & (spot < line - 1))
        def _():
            send_up(block).wait_send()

        @pl.when((place >= spot) & (spot > 0))
        def _():
            send_down(block).wait_send()

        send_side(block).wait_send()
        return carry

    def settle_blk(step, carry):
        peer = lax.rem(blk + step, blocks)
        send_foot(peer).wait_send()
        cut_copy(peer, blk).wait_send()
        return carry

    def settle_gy(step, carry):
        part_copy(lax.rem(gy + step, groups), gy).wait_send()
        return carry

    lax.fori_loop(0, line, settle_line, 0)
    lax.fori_loop(1, blocks, settle_blk, 0)
    lax.fori_loop(1, groups, settle_gy, 0)


def per_device(blocks, groups, image, measured, row_weight, col_weight, band_weight, band_shift):
    _, col_count, depth = image.shape
    local_tilts, _, band_width = band_weight.shape
    detector_len = measured.shape[2]
    reach = (col_count // PW + SHIFTS) * PW
    window = (blocks, local_tilts, reach)
    dma = pltpu.SemaphoreType.DMA
    updated = pl.pallas_call(
        functools.partial(kernel, blocks, groups),
        out_shape=jax.ShapeDtypeStruct((col_count, depth), jnp.float32),
        in_specs=[pl.BlockSpec(memory_space=pltpu.VMEM)] * 6,
        out_specs=pl.BlockSpec(memory_space=pltpu.VMEM),
        scratch_shapes=[
            pltpu.VMEM((blocks,) + band_weight.shape, jnp.bfloat16),
            pltpu.VMEM((col_count, depth), jnp.bfloat16),
            pltpu.VMEM((blocks * local_tilts, PW), jnp.int32),
            pltpu.VMEM(window, jnp.float32),
            pltpu.VMEM(window, jnp.float32),
            pltpu.VMEM((groups, local_tilts, detector_len), jnp.float32),
            pltpu.VMEM(window, jnp.float32),
            pltpu.VMEM(window, jnp.float32),
            pltpu.VMEM((2, 8, col_count), jnp.float32),
            pltpu.VMEM((2, PW, col_count), jnp.float32),
            dma((blocks,)), dma((blocks,)), dma((blocks,)), dma((blocks,)),
            dma((blocks,)), dma((blocks,)), dma((groups,)), dma((groups,)),
            dma((blocks,)), dma((blocks,)), dma((2,)), dma((2,)),
        ],
        compiler_params=pltpu.CompilerParams(
            collective_id=0, has_side_effects=True, vmem_limit_bytes=40 * 1024 * 1024
        ),
        cost_estimate=pl.CostEstimate(
            flops=4 * blocks * local_tilts * band_width * col_count * depth,
            bytes_accessed=12 * col_count * depth,
            transcendentals=0,
        ),
    )(image[0], measured[0], row_weight, col_weight, band_weight, band_shift)
    return updated[None]


def solution(mesh):
    return jax.shard_map(
        functools.partial(per_device, mesh.shape["blk"], mesh.shape["gy"]),
        mesh=mesh,
        in_specs=(
            P(None, "blk", "gy"),
            P(None, "blk", None),
            P("blk", None),
            P("blk", "gy"),
            P("blk", "gy", None),
            P(),
        ),
        out_specs=P(None, "blk", "gy"),
        check_vma=False,
    )
```

time: 205 us -> 53.7 us (0.26)
  waiting for transfers between devices: 57.6 us -> 0 us
  Pallas kernels: 0 us -> 47.2 us
  local copies, waits for them, and re-layouts: 49.3 us -> 6.05 us
  loops' own time: 28.2 us -> 0 us
  other arithmetic: 25.6 us -> 0 us
  between operations: 13.6 us -> 0.01 us
  starting transfers between devices: 11.1 us -> 0 us
  blocking collectives: 10.3 us -> 0 us
  matrix products: 8.25 us -> 0 us
    pallas_call x0 -> x1, Pallas kernels: none -> 47.2 us  [per_device(): pl.pallas_call(functools.partial(kernel, blocks, groups), out_shape=jax.S...]
    all_gather x1 -> x0, waiting for transfers between devices: 46 us -> none  [per_device(): all_weights = lax.all_gather(band_weight, 'blk', axis=0, tiled=True)]
    another operation x5 -> x0, loops' own time: 28.2 us -> none  [the longest x1 27.2 us: per_device(): partial_sum = lax.fori_loop(0, block_count, add_source, initial)]
    gather x64 -> x0, local copies, waits for them, and re-layouts: 22.3 us -> none
    slice x62 -> x0, local copies, waits for them, and re-layouts: 16.6 us -> none  [the longest x60 15.1 us: shift_rows(): moved = jnp.roll(rows, direction * (1 << level), axis=-1)]
    select_n x29 -> x0, other arithmetic: 16.4 us -> none  [the longest x28 16.4 us: shift_rows(): rows = jnp.where(chosen, moved, rows)]
    all_to_all x2 -> x0, waiting for transfers between devices: 10.8 us -> none  [the longest x1 6.42 us: per_device(): lax.all_to_all(windows, 'blk', split_axis=0, concat_axis=0, tiled=True)]
    psum x1 -> x0, blocking collectives: 10.3 us -> none  [per_device(): projection = lax.psum(partial_sum, 'gy')]
  transfers between devices with their start and end apart: 5 -> 0, of which waited for: 3 -> 0; matrix products, arithmetic and copies ran while one was open for 25% -> 0% of each run, Pallas kernels for 0% -> 0%
where the time goes in v1:
time: 53.7 us; the launch traced here: 53.3 us
  Pallas kernels  47.2 us (88%)
  local copies, waits for them, and re-layouts  6.05 us (11%)
    pallas_call x1, Pallas kernels, per_device(): pl.pallas_call(functools.partial(kernel, blocks, groups), out_shape=jax.S...  47.2 us
    unnamed x12, local copies, waits for them, and re-layouts  6.05 us

profile of v1, /device:TPU:0, one launch (start us, length us, event | category | flops | bytes accessed | tf_op | source)
XLA Modules:
  0.0 53.3 jit_solution(16376146740277157476)
XLA Ops:
  0.0 0.8 %copy.7.shift_ref = s32[16,8]{1,0:T(8,128)S(1)} copy(s32[16,8]{0,1:T(8,128)} %param.11) | data formatting | bytes 1024 | tf_op args[5]
  0.8 0.0 copy-start
  0.8 1.0 %copy-done = f32[1,256,512]{2,1,0:T(8,128)S(1)} copy-done((f32[1,256,512]{2,1,0:T(8,128)S(1)}, f32[1,256,512]{2,1,0:T(8,128)}, u32[]{:S(2)}) %copy-start) | copy-done | bytes 524312
  1.8 0.0 copy-start.1
  1.8 1.0 %copy-done.1 = f32[256,512]{1,0:T(8,128)S(1)} copy-done((f32[256,512]{1,0:T(8,128)S(1)}, f32[256,512]{1,0:T(8,128)}, u32[]{:S(2)}) %copy-start.1) | copy-done | bytes 524312
  2.8 0.0 copy-start.2
  2.8 0.9 %copy-done.2 = bf16[2,512,128]{2,1,0:T(8,128)(2,1)S(1)} copy-done((bf16[2,512,128]{2,1,0:T(8,128)(2,1)S(1)}, bf16[2,512,128]{2,1,0:T(8,128)(2,1)}, u32[]{:S(2)}) %copy-start.2) | copy-done | bytes 262168
  3.8 0.0 copy-start.3
  3.8 0.7 %copy-done.3 = f32[1,2,2816]{2,1,0:T(2,128)S(1)} copy-done((f32[1,2,2816]{2,1,0:T(2,128)S(1)}, f32[1,2,2816]{2,1,0:T(2,128)}, u32[]{:S(2)}) %copy-start.3) | copy-done | bytes 22552
  4.5 0.0 copy-start.4
  4.5 0.7 %copy-done.4 = f32[2,2816]{1,0:T(2,128)S(1)} copy-done((f32[2,2816]{1,0:T(2,128)S(1)}, f32[2,2816]{1,0:T(2,128)}, u32[]{:S(2)}) %copy-start.4) | copy-done | bytes 22552
  5.3 47.2 %shard_map.64 = f32[256,512]{1,0:T(8,128)S(1)} custom-call(f32[256,512]{1,0:T(8,128)S(1)} %bitcast.4, f32[2,2816]{1,0:T(2,128)S(1)} %bitcast.5, f32[2,2816]{1,0:T(2,128)S(1)} %copy-done.4, f32[256,512]{1,0:T(8,128)S(1)} %copy-done.1, bf16[2,512,128]{2,1,0:T(8,128)(2,1)S(1)} %copy-done.2, s32[16,8]{1,0:T(8,128)S(1)} %copy.7.shift_ref), custom_call_target="tpu_custom_call" | custom-call | flops 1073741824 | bytes 1572864 | tf_op jit(solution)/shard_map/pallas_call | solution.py:363
  52.5 0.8 %copy.9 = f32[1,256,512]{2,1,0:T(8,128)} copy(f32[1,256,512]{2,1,0:T(8,128)S(1)} %bitcast.3) | data formatting | bytes 1048576
Async XLA Ops:
  0.8 1.0 %copy-start = (f32[1,256,512]{2,1,0:T(8,128)S(1)}, f32[1,256,512]{2,1,0:T(8,128)}, u32[]{:S(2)}) copy-start(f32[1,256,512]{2,1,0:T(8,128)} %param.6) | copy-start | bytes 1572868
  1.8 1.0 %copy-start.1 = (f32[256,512]{1,0:T(8,128)S(1)}, f32[256,512]{1,0:T(8,128)}, u32[]{:S(2)}) copy-start(f32[256,512]{1,0:T(8,128)} %col_ref.1) | copy-start | bytes 1572868
  2.8 0.9 %copy-start.2 = (bf16[2,512,128]{2,1,0:T(8,128)(2,1)S(1)}, bf16[2,512,128]{2,1,0:T(8,128)(2,1)}, u32[]{:S(2)}) copy-start(bf16[2,512,128]{2,1,0:T(8,128)(2,1)} %band_ref.1) | copy-start | bytes 786436
  3.8 0.7 %copy-start.3 = (f32[1,2,2816]{2,1,0:T(2,128)S(1)}, f32[1,2,2816]{2,1,0:T(2,128)}, u32[]{:S(2)}) copy-start(f32[1,2,2816]{2,1,0:T(2,128)} %param.7) | copy-start | bytes 67588
  4.5 0.7 %copy-start.4 = (f32[2,2816]{1,0:T(2,128)S(1)}, f32[2,2816]{1,0:T(2,128)}, u32[]{:S(2)}) copy-start(f32[2,2816]{1,0:T(2,128)} %row_ref.1) | copy-start | bytes 67588

commit v2 on v1

--- a/solution.py
+++ b/solution.py
@@ -42,21 +42,36 @@
 
 def kernel(
     blocks, groups,
-    image_ref, measured_ref, row_ref, col_ref, band_ref, shift_ref, out_ref,
-    weights, copies, shift_rows, placed, footprints, partial, cut, panels, edge_out, edge_in,
+    image_hbm, measured_hbm, row_hbm, col_hbm, band_ref, shift_ref, out_ref,
+    image_ref, measured_ref, row_ref, col_ref, weights, copies, shift_rows, placed, footprints, partial, cut, panels, edge_out, edge_in,
     up_sem, down_sem, side_sem, weight_sem,
     foot_send, foot_recv, part_send, part_recv, cut_send, cut_recv, edge_send, edge_recv,
+    load_sem,
 ):
     blk, gy = lax.axis_index("blk"), lax.axis_index("gy")
     line = blocks // 2
     spot, side = blk // 2, blk % 2
     local_tilts, depth, band_width = band_ref.shape
-    col_count = image_ref.shape[0]
+    col_count = image_hbm.shape[0]
     detector_len = measured_ref.shape[1]
     per_slab = col_count // PW
     window_panels = per_slab + 1
     reach = window_panels + SHIFTS - 1
 
+    loads = [
+        pltpu.make_async_copy(source, target, load_sem.at[number])
+        for number, (source, target) in enumerate(
+            [
+                (image_hbm, image_ref),
+                (band_ref, weights.at[blk]),
+                (measured_hbm, measured_ref),
+                (row_hbm, row_ref),
+                (col_hbm, col_ref),
+            ]
+        )
+    ]
+    for load in loads:
+        load.start()
     edge_in[...] = jnp.zeros_like(edge_in)
     barrier = pltpu.get_barrier_semaphore()
 
@@ -74,21 +89,22 @@
     lax.fori_loop(1, groups, greet_gy, 0)
     pl.semaphore_wait(barrier, blocks + groups - 2)
 
-    def send_weights(block, sems, to):
-        return pltpu.make_async_remote_copy(
-            src_ref=weights.at[block], dst_ref=weights.at[block],
-            send_sem=sems.at[block], recv_sem=weight_sem.at[block],
+    def send_weights(block, tilt, sems, to, source):
+        held = weights.at[block, tilt]
+        return pltpu.make_async_remote_copy(
+            src_ref=held if source is None else source.at[tilt], dst_ref=held,
+            send_sem=sems.at[block, tilt], recv_sem=weight_sem.at[block, tilt],
             device_id=(to, gy), device_id_type=MESH,
         )
 
-    def send_up(block):
-        return send_weights(block, up_sem, lax.rem(blk + 2, blocks))
-
-    def send_down(block):
-        return send_weights(block, down_sem, lax.rem(blk + blocks - 2, blocks))
-
-    def send_side(block):
-        return send_weights(block, side_sem, blk + 1 - 2 * side)
+    def send_up(block, tilt, source=None):
+        return send_weights(block, tilt, up_sem, lax.rem(blk + 2, blocks), source)
+
+    def send_down(block, tilt, source=None):
+        return send_weights(block, tilt, down_sem, lax.rem(blk + blocks - 2, blocks), source)
+
+    def send_side(block, tilt, source=None):
+        return send_weights(block, tilt, side_sem, blk + 1 - 2 * side, source)
 
     def send_foot(block):
         return pltpu.make_async_remote_copy(
@@ -117,21 +133,30 @@
     def head_copy():
         return edge_copy(1, lax.rem(gy + groups - 1, groups))
 
-    weights[blk] = band_ref[...]
-
-    @pl.when(spot < line - 1)
-    def _():
-        send_up(blk).start()
-
-    @pl.when(spot > 0)
-    def _():
-        send_down(blk).start()
-
-    send_side(blk).start()
-
+    last = local_tilts - 1
+    can_up, can_down = spot < line - 1, spot > 0
+    for tilt in range(local_tilts):
+
+        @pl.when(can_up)
+        def _():
+            send_up(blk, tilt, band_ref).start()
+
+        @pl.when(can_down)
+        def _():
+            send_down(blk, tilt, band_ref).start()
+
+        send_side(blk, tilt, band_ref).start()
+
+    loads[0].wait()
     copies[...] = image_ref[...].astype(jnp.bfloat16)
-    slab = lax.broadcasted_iota(jnp.int32, shift_ref.shape, 1)
-    own_shift = jnp.sum(jnp.where(slab == blk, shift_ref[...], 0), axis=1, keepdims=True)
+    slab = lax.broadcasted_iota(jnp.int32, shift_ref.shape, 0)
+    own_shift = jnp.sum(jnp.where(slab == blk, shift_ref[...], 0), axis=0, keepdims=True)
+    square = (blocks * local_tilts, blocks * local_tilts)
+    diagonal = lax.broadcasted_iota(jnp.int32, square, 0) == lax.broadcasted_iota(
+        jnp.int32, square, 1
+    )
+    own_shift = jnp.where(diagonal, jnp.broadcast_to(own_shift, square), 0)
+    own_shift = jnp.sum(own_shift, axis=1, keepdims=True)
     shift_rows[...] = jnp.broadcast_to(own_shift, shift_rows.shape)
 
     edge_out[0] = image_ref[:, depth - PW :].T[PW - 8 :]
@@ -148,18 +173,21 @@
     def wide(block):
         return jnp.concatenate([weights[block, t] for t in range(local_tilts)], axis=1)
 
-    def project(block):
-        product = jnp.dot(copies[...], wide(block), preferred_element_type=jnp.float32)
-        for t in range(local_tilts):
-            window = diagonal_sum(product[:, t * band_width : (t + 1) * band_width])
-            shift = shift_rows[pl.ds(block * local_tilts + t, 1), :]
-            for panel in range(reach):
-                total = jnp.zeros((1, PW), jnp.float32)
-                for k in range(SHIFTS):
-                    if 0 <= panel - k < window_panels:
-                        piece = window[:, (panel - k) * PW : (panel - k + 1) * PW]
-                        total = jnp.where(shift == k, piece, total)
-                placed[block, pl.ds(t, 1), pl.ds(panel * PW, PW)] = total
+    def project(block, tilt):
+        product = jnp.dot(
+            copies[...], weights[block, tilt], preferred_element_type=jnp.float32
+        )
+        window = diagonal_sum(product)
+        shift = shift_rows[pl.ds(block * local_tilts + tilt, 1), :]
+        for panel in range(reach):
+            total = jnp.zeros((1, PW), jnp.float32)
+            for k in range(SHIFTS):
+                if 0 <= panel - k < window_panels:
+                    piece = window[:, (panel - k) * PW : (panel - k + 1) * PW]
+                    total = jnp.where(shift == k, piece, total)
+            placed[block, pl.ds(tilt, 1), pl.ds(panel * PW, PW)] = total
+        if tilt < last:
+            return
 
         @pl.when(block != blk)
         def _():
@@ -168,51 +196,75 @@
         @pl.when(block == blk)
         def _():
             footprints[blk] = placed[blk]
+
+    partner = blk + 1 - 2 * side
+    handover = max(line - 1, 2)
 
     def gather_step(step, carry):
         below, above = spot - step, spot + step
 
-        @pl.when((step > 0) & (below >= 0))
-        def _():
-            block = below * 2 + side
-            send_up(block).wait_recv()
-
-            @pl.when(spot < line - 1)
+        @pl.when((step == handover) & can_up)
+        def _():
+            send_up(partner, last).start()
+
+        @pl.when((step == handover) & can_down)
+        def _():
+            send_down(partner, last).start()
+
+        for tilt in range(local_tilts):
+            across = (step > 1) | (tilt < last)
+
+            @pl.when((step > 0) & (below >= 0))
             def _():
-                send_up(block).start()
-
-            send_side(block).start()
-
-        @pl.when((step > 0) & (above < line))
-        def _():
-            block = above * 2 + side
-            send_down(block).wait_recv()
-
-            @pl.when(spot > 0)
+                block = below * 2 + side
+                send_up(block, tilt).wait_recv()
+
+                @pl.when(can_up)
+                def _():
+                    send_up(block, tilt).start()
+
+                @pl.when(across)
+                def _():
+                    send_side(block, tilt).start()
+
+            @pl.when((step > 0) & (above < line))
             def _():
-                send_down(block).start()
-
-            send_side(block).start()
+                block = above * 2 + side
+                send_down(block, tilt).wait_recv()
+
+                @pl.when(can_down)
+                def _():
+                    send_down(block, tilt).start()
+
+                @pl.when(across)
+                def _():
+                    send_side(block, tilt).start()
 
         def visit(turn, carry):
-            other = turn // 2
-            far = step - other
+            kind = turn // 2
+            far = jnp.where(kind == 2, 1, step - kind)
             place = jnp.where(turn % 2 == 0, spot - far, spot + far)
             inside = (far >= 0) & (place >= 0) & (place < line) & ((far > 0) | (turn % 2 == 0))
-            block = place * 2 + jnp.where(other == 0, side, 1 - side)
-
-            @pl.when(inside)
-            def _():
-                @pl.when(other == 1)
+            inside = inside & ((kind < 2) | (step == line))
+            block = place * 2 + jnp.where(kind == 0, side, 1 - side)
+            late = (kind == 1) & (far == 1)
+            for tilt in range(local_tilts):
+                wanted = ~late & (kind < 2) if tilt == last else kind < 2
+                wanted = wanted | (kind == 2) if tilt == last else wanted
+
+                @pl.when(inside & wanted)
                 def _():
-                    send_side(block).wait_recv()
-
-                project(block)
+                    @pl.when(kind > 0)
+                    def _():
+                        send_side(block, tilt).wait_recv()
+
+                    project(block, tilt)
 
             return carry
 
-        return lax.fori_loop(0, 4, visit, carry)
-
+        return lax.fori_loop(0, 6, visit, carry)
+
+    loads[1].wait()
     lax.fori_loop(0, line + 1, gather_step, 0)
 
     def take_foot(step, carry):
@@ -245,6 +297,8 @@
     lax.fori_loop(1, groups, give_part, 0)
     lax.fori_loop(1, groups, take_part, 0)
 
+    loads[2].wait()
+    loads[3].wait()
     projection = partial[0]
     for group in range(1, groups):
         projection = projection + partial[group]
@@ -303,6 +357,7 @@
     def _():
         head_copy().wait_recv()
 
+    loads[4].wait()
     before = edge_in[0].T[:, 7:8]
     after = edge_in[1].T[:, 0:1]
     chunk = 32
@@ -326,17 +381,31 @@
 
     def settle_line(place, carry):
         block = place * 2 + side
-
-        @pl.when((place <= spot) & (spot < line - 1))
-        def _():
-            send_up(block).wait_send()
-
-        @pl.when((place >= spot) & (spot > 0))
-        def _():
-            send_down(block).wait_send()
-
-        send_side(block).wait_send()
-        return carry
+        for tilt in range(local_tilts):
+
+            @pl.when((place <= spot) & can_up)
+            def _():
+                send_up(block, tilt).wait_send()
+
+            @pl.when((place >= spot) & can_down)
+            def _():
+                send_down(block, tilt).wait_send()
+
+            near = (place == spot - 1) | (place == spot + 1)
+
+            @pl.when(~near | (tilt < last))
+            def _():
+                send_side(block, tilt).wait_send()
+
+        return carry
+
+    @pl.when(can_up)
+    def _():
+        send_up(partner, last).wait_send()
+
+    @pl.when(can_down)
+    def _():
+        send_down(partner, last).wait_send()
 
     def settle_blk(step, carry):
         peer = lax.rem(blk + step, blocks)
@@ -360,12 +429,18 @@
     reach = (col_count // PW + SHIFTS) * PW
     window = (blocks, local_tilts, reach)
     dma = pltpu.SemaphoreType.DMA
+    units = dma((blocks, local_tilts))
     updated = pl.pallas_call(
         functools.partial(kernel, blocks, groups),
         out_shape=jax.ShapeDtypeStruct((col_count, depth), jnp.float32),
-        in_specs=[pl.BlockSpec(memory_space=pltpu.VMEM)] * 6,
+        in_specs=[pl.BlockSpec(memory_space=pl.ANY)] * 5
+        + [pl.BlockSpec(memory_space=pltpu.VMEM)],
         out_specs=pl.BlockSpec(memory_space=pltpu.VMEM),
         scratch_shapes=[
+            pltpu.VMEM((col_count, depth), jnp.float32),
+            pltpu.VMEM((local_tilts, detector_len), jnp.float32),
+            pltpu.VMEM((local_tilts, detector_len), jnp.float32),
+            pltpu.VMEM((col_count, depth), jnp.float32),
             pltpu.VMEM((blocks,) + band_weight.shape, jnp.bfloat16),
             pltpu.VMEM((col_count, depth), jnp.bfloat16),
             pltpu.VMEM((blocks * local_tilts, PW), jnp.int32),
@@ -376,19 +451,19 @@
             pltpu.VMEM(window, jnp.float32),
             pltpu.VMEM((2, 8, col_count), jnp.float32),
             pltpu.VMEM((2, PW, col_count), jnp.float32),
-            dma((blocks,)), dma((blocks,)), dma((blocks,)), dma((blocks,)),
+            units, units, units, units,
             dma((blocks,)), dma((blocks,)), dma((groups,)), dma((groups,)),
-            dma((blocks,)), dma((blocks,)), dma((2,)), dma((2,)),
+            dma((blocks,)), dma((blocks,)), dma((2,)), dma((2,)), dma((5,)),
         ],
         compiler_params=pltpu.CompilerParams(
-            collective_id=0, has_side_effects=True, vmem_limit_bytes=40 * 1024 * 1024
+            collective_id=0, has_side_effects=True, vmem_limit_bytes=56 * 1024 * 1024
         ),
         cost_estimate=pl.CostEstimate(
             flops=4 * blocks * local_tilts * band_width * col_count * depth,
             bytes_accessed=12 * col_count * depth,
             transcendentals=0,
         ),
-    )(image[0], measured[0], row_weight, col_weight, band_weight, band_shift)
+    )(image[0], measured[0], row_weight, col_weight, band_weight, band_shift.T)
     return updated[None]
 
 

time: 53.7 us -> 49.9 us (0.929)
  local copies, waits for them, and re-layouts: 6.05 us -> 1.87 us
  Pallas kernels: 47.2 us -> 47.8 us
    unnamed x12 -> x1, local copies, waits for them, and re-layouts: 6.05 us -> 1.87 us
    pallas_call x1, Pallas kernels: 47.2 us -> 47.8 us  [per_device(): pl.pallas_call(functools.partial(kernel, blocks, groups), out_shape=jax.S...]
where the time goes in v2:
time: 49.9 us; the launch traced here: 49.7 us
  Pallas kernels  47.8 us (96%)
  local copies, waits for them, and re-layouts  1.87 us (4%)
    pallas_call x1, Pallas kernels, per_device(): pl.pallas_call(functools.partial(kernel, blocks, groups), out_shape=jax.S...  47.8 us
    unnamed x1, local copies, waits for them, and re-layouts  1.87 us

profile of v2, /device:TPU:0, one launch (start us, length us, event | category | flops | bytes accessed | tf_op | source)
XLA Modules:
  0.0 49.7 jit_solution(5250277170800831424)
XLA Ops:
  0.0 47.8 %shard_map.64 = f32[256,512]{1,0:T(8,128)} custom-call(f32[256,512]{1,0:T(8,128)} %bitcast.5, f32[2,2816]{1,0:T(2,128)} %bitcast.6, f32[2,2816]{1,0:T(2,128)} %row_hbm.1, f32[256,512]{1,0:T(8,128)} %col_hbm.1, bf16[2,512,128]{2,1,0:T(8,128)(2,1)} %band_ref.1, s32[8,16]{1,0:T(8,128)} %bitcast.7), custom_call_target="tpu_custom_call" | custom-call | flops 1073741824 | bytes 1572864 | tf_op jit(solution)/shard_map/pallas_call | solution.py:433
  47.8 1.9 %copy.8 = f32[1,256,512]{2,1,0:T(8,128)} copy(f32[1,256,512]{2,1,0:T(8,128)} %bitcast.4) | data formatting | bytes 1048576

commit v3 on v2

--- a/solution.py
+++ b/solution.py
@@ -432,7 +432,7 @@
     units = dma((blocks, local_tilts))
     updated = pl.pallas_call(
         functools.partial(kernel, blocks, groups),
-        out_shape=jax.ShapeDtypeStruct((col_count, depth), jnp.float32),
+        out_shape=pltpu.VMEM((col_count, depth), jnp.float32),
         in_specs=[pl.BlockSpec(memory_space=pl.ANY)] * 5
         + [pl.BlockSpec(memory_space=pltpu.VMEM)],
         out_specs=pl.BlockSpec(memory_space=pltpu.VMEM),

time: 49.9 us -> 48 us (0.962)
  local copies, waits for them, and re-layouts: 1.87 us -> 0.8 us
  Pallas kernels: 47.8 us -> 47 us
    unnamed x1, local copies, waits for them, and re-layouts: 1.87 us -> 0.8 us
    pallas_call x1, Pallas kernels: 47.8 us -> 47 us  [per_device(): pl.pallas_call(functools.partial(kernel, blocks, groups), out_shape=pltpu...]
where the time goes in v3:
time: 48 us; the launch traced here: 47.8 us
  Pallas kernels  47 us (98%)
  local copies, waits for them, and re-layouts  0.8 us (2%)
    pallas_call x1, Pallas kernels, per_device(): pl.pallas_call(functools.partial(kernel, blocks, groups), out_shape=pltpu...  47 us

profile of v3, /device:TPU:0, one launch (start us, length us, event | category | flops | bytes accessed | tf_op | source)
XLA Modules:
  0.0 47.8 jit_solution(9766297474098928861)
XLA Ops:
  0.0 47.0 %shard_map.64 = f32[256,512]{1,0:T(8,128)S(1)} custom-call(f32[256,512]{1,0:T(8,128)} %bitcast.5, f32[2,2816]{1,0:T(2,128)} %bitcast.6, f32[2,2816]{1,0:T(2,128)} %row_hbm.1, f32[256,512]{1,0:T(8,128)} %col_hbm.1, bf16[2,512,128]{2,1,0:T(8,128)(2,1)} %band_ref.1, s32[8,16]{1,0:T(8,128)} %bitcast.7), custom_call_target="tpu_custom_call" | custom-call | flops 1073741824 | bytes 1572864 | tf_op jit(solution)/shard_map/pallas_call | solution.py:433
  47.0 0.8 %copy.8 = f32[1,256,512]{2,1,0:T(8,128)} copy(f32[1,256,512]{2,1,0:T(8,128)S(1)} %bitcast.4) | data formatting | bytes 1048576

commit v4 on v3

--- a/solution.py
+++ b/solution.py
@@ -1,4 +1,5 @@
 import functools
+import math
 
 import jax
 import jax.numpy as jnp
@@ -43,7 +44,7 @@
 def kernel(
     blocks, groups,
     image_hbm, measured_hbm, row_hbm, col_hbm, band_ref, shift_ref, out_ref,
-    image_ref, measured_ref, row_ref, col_ref, weights, copies, shift_rows, placed, footprints, partial, cut, panels, edge_out, edge_in,
+    image_ref, measured_ref, row_ref, col_ref, weights, wide, sheared, copies, shift_rows, placed, footprints, partial, cut, panels, edge_out, edge_in,
     up_sem, down_sem, side_sem, weight_sem,
     foot_send, foot_recv, part_send, part_recv, cut_send, cut_recv, edge_send, edge_recv,
     load_sem,
@@ -170,13 +171,14 @@
     def _():
         head_copy().start()
 
-    def wide(block):
-        return jnp.concatenate([weights[block, t] for t in range(local_tilts)], axis=1)
+    def lanes_of(block, tilt):
+        number = block * local_tilts + tilt
+        return pl.ds(pl.multiple_of(number * band_width, band_width), band_width)
 
     def project(block, tilt):
-        product = jnp.dot(
-            copies[...], weights[block, tilt], preferred_element_type=jnp.float32
-        )
+        band = weights[block, tilt]
+        wide[:, lanes_of(block, tilt)] = band
+        product = jnp.dot(copies[...], band, preferred_element_type=jnp.float32)
         window = diagonal_sum(product)
         shift = shift_rows[pl.ds(block * local_tilts + tilt, 1), :]
         for panel in range(reach):
@@ -197,6 +199,26 @@
         def _():
             footprints[blk] = placed[blk]
 
+    def smooth():
+        @pl.when(gy > 0)
+        def _():
+            tail_copy().wait_recv()
+
+        @pl.when(gy < groups - 1)
+        def _():
+            head_copy().wait_recv()
+
+        before = edge_in[0].T[:, 7:8]
+        after = edge_in[1].T[:, 0:1]
+        chunk = 32
+        lane = lax.broadcasted_iota(jnp.int32, (chunk, depth), 1)
+        for top in range(0, col_count, chunk):
+            rows = slice(top, top + chunk)
+            here = image_ref[rows, :]
+            left = jnp.where(lane == 0, before[rows], roll_lanes(here, 1))
+            right = jnp.where(lane == depth - 1, after[rows], roll_lanes(here, -1))
+            out_ref[rows, :] = here + SMOOTH * (left + right - 2.0 * here)
+
     partner = blk + 1 - 2 * side
     handover = max(line - 1, 2)
 
@@ -262,7 +284,13 @@
 
             return carry
 
-        return lax.fori_loop(0, 6, visit, carry)
+        lax.fori_loop(0, 6, visit, 0)
+
+        @pl.when(step == line)
+        def _():
+            smooth()
+
+        return carry
 
     loads[1].wait()
     lax.fori_loop(0, line + 1, gather_step, 0)
@@ -321,55 +349,36 @@
 
     lax.fori_loop(1, blocks, give_cut, 0)
     panels[blk] = cut[blk]
-    out_ref[...] = jnp.zeros_like(out_ref)
+
+    batch = math.gcd(blocks, 4)
 
     def back_step(step, carry):
-        source = lax.rem(blk + step, blocks)
-
-        @pl.when(step > 0)
-        def _():
-            cut_copy(source, source).wait_recv()
-
-        sheared = []
-        for t in range(local_tilts):
-            shift = shift_rows[pl.ds(source * local_tilts + t, 1), :]
-            pieces = []
-            for panel in range(window_panels):
-                piece = panels[source, pl.ds(t, 1), pl.ds(panel * PW, PW)]
-                for k in range(1, SHIFTS):
-                    moved = panels[source, pl.ds(t, 1), pl.ds((panel + k) * PW, PW)]
-                    piece = jnp.where(shift == k, moved, piece)
-                pieces.append(piece)
-            sheared.append(band_rows(jnp.concatenate(pieces, axis=1), col_count))
-        rows = jnp.concatenate(sheared, axis=1).astype(jnp.bfloat16)
-        out_ref[...] += lax.dot_general(
-            rows, wide(source), (((1,), (1,)), ((), ())), preferred_element_type=jnp.float32
-        )
-        return carry
-
-    lax.fori_loop(0, blocks, back_step, 0)
-
-    @pl.when(gy > 0)
-    def _():
-        tail_copy().wait_recv()
-
-    @pl.when(gy < groups - 1)
-    def _():
-        head_copy().wait_recv()
-
+        sources = [lax.rem(blk + step * batch + number, blocks) for number in range(batch)]
+        for number, source in enumerate(sources):
+
+            @pl.when(step + number > 0)
+            def _():
+                cut_copy(source, source).wait_recv()
+
+        for source in sources:
+            for t in range(local_tilts):
+                shift = shift_rows[pl.ds(source * local_tilts + t, 1), :]
+                pieces = []
+                for panel in range(window_panels):
+                    piece = panels[source, pl.ds(t, 1), pl.ds(panel * PW, PW)]
+                    for k in range(1, SHIFTS):
+                        moved = panels[source, pl.ds(t, 1), pl.ds((panel + k) * PW, PW)]
+                        piece = jnp.where(shift == k, moved, piece)
+                    pieces.append(piece)
+                rows = band_rows(jnp.concatenate(pieces, axis=1), col_count)
+                sheared[:, lanes_of(source, t)] = rows.astype(jnp.bfloat16)
+        return carry
+
+    lax.fori_loop(0, blocks // batch, back_step, 0)
     loads[4].wait()
-    before = edge_in[0].T[:, 7:8]
-    after = edge_in[1].T[:, 0:1]
-    chunk = 32
-    lane = lax.broadcasted_iota(jnp.int32, (chunk, depth), 1)
-    for top in range(0, col_count, chunk):
-        rows = slice(top, top + chunk)
-        here = image_ref[rows, :]
-        left = jnp.where(lane == 0, before[rows], roll_lanes(here, 1))
-        right = jnp.where(lane == depth - 1, after[rows], roll_lanes(here, -1))
-        out_ref[rows, :] = (
-            here + col_ref[rows, :] * out_ref[rows, :] + SMOOTH * (left + right - 2.0 * here)
-        )
+    out_ref[...] += col_ref[...] * lax.dot_general(
+        sheared[...], wide[...], (((1,), (1,)), ((), ())), preferred_element_type=jnp.float32
+    )
 
     @pl.when(gy < groups - 1)
     def _():
@@ -442,6 +451,8 @@
             pltpu.VMEM((local_tilts, detector_len), jnp.float32),
             pltpu.VMEM((col_count, depth), jnp.float32),
             pltpu.VMEM((blocks,) + band_weight.shape, jnp.bfloat16),
+            pltpu.VMEM((depth, blocks * local_tilts * band_width), jnp.bfloat16),
+            pltpu.VMEM((col_count, blocks * local_tilts * band_width), jnp.bfloat16),
             pltpu.VMEM((col_count, depth), jnp.bfloat16),
             pltpu.VMEM((blocks * local_tilts, PW), jnp.int32),
             pltpu.VMEM(window, jnp.float32),

time: 48 us -> 46.1 us (0.960)
  Pallas kernels: 47 us -> 45.1 us
    pallas_call x1, Pallas kernels: 47 us -> 45.1 us  [per_device(): pl.pallas_call(functools.partial(kernel, blocks, groups), out_shape=pltpu...]
where the time goes in v4:
time: 46.1 us; the launch traced here: 45.9 us
  Pallas kernels  45.1 us (98%)
  local copies, waits for them, and re-layouts  0.8 us (2%)
    pallas_call x1, Pallas kernels, per_device(): pl.pallas_call(functools.partial(kernel, blocks, groups), out_shape=pltpu...  45.1 us

profile of v4, /device:TPU:0, one launch (start us, length us, event | category | flops | bytes accessed | tf_op | source)
XLA Modules:
  0.0 45.9 jit_solution(18223225956281776712)
XLA Ops:
  0.0 45.1 %shard_map.64 = f32[256,512]{1,0:T(8,128)S(1)} custom-call(f32[256,512]{1,0:T(8,128)} %bitcast.5, f32[2,2816]{1,0:T(2,128)} %bitcast.6, f32[2,2816]{1,0:T(2,128)} %row_hbm.1, f32[256,512]{1,0:T(8,128)} %col_hbm.1, bf16[2,512,128]{2,1,0:T(8,128)(2,1)} %band_ref.1, s32[8,16]{1,0:T(8,128)} %bitcast.7), custom_call_target="tpu_custom_call" | custom-call | flops 1073741824 | bytes 1572864 | tf_op jit(solution)/shard_map/pallas_call | solution.py:442
  45.1 0.8 %copy.8 = f32[1,256,512]{2,1,0:T(8,128)} copy(f32[1,256,512]{2,1,0:T(8,128)S(1)} %bitcast.4) | data formatting | bytes 1048576

commit v5 on v4

--- a/solution.py
+++ b/solution.py
@@ -374,6 +374,35 @@
                 sheared[:, lanes_of(source, t)] = rows.astype(jnp.bfloat16)
         return carry
 
+    def settle_line(place, carry):
+        block = place * 2 + side
+        for tilt in range(local_tilts):
+
+            @pl.when((place <= spot) & can_up)
+            def _():
+                send_up(block, tilt).wait_send()
+
+            @pl.when((place >= spot) & can_down)
+            def _():
+                send_down(block, tilt).wait_send()
+
+            near = (place == spot - 1) | (place == spot + 1)
+
+            @pl.when(~near | (tilt < last))
+            def _():
+                send_side(block, tilt).wait_send()
+
+        return carry
+
+    @pl.when(can_up)
+    def _():
+        send_up(partner, last).wait_send()
+
+    @pl.when(can_down)
+    def _():
+        send_down(partner, last).wait_send()
+
+    lax.fori_loop(0, line, settle_line, 0)
     lax.fori_loop(0, blocks // batch, back_step, 0)
     loads[4].wait()
     out_ref[...] += col_ref[...] * lax.dot_general(
@@ -388,34 +417,6 @@
     def _():
         head_copy().wait_send()
 
-    def settle_line(place, carry):
-        block = place * 2 + side
-        for tilt in range(local_tilts):
-
-            @pl.when((place <= spot) & can_up)
-            def _():
-                send_up(block, tilt).wait_send()
-
-            @pl.when((place >= spot) & can_down)
-            def _():
-                send_down(block, tilt).wait_send()
-
-            near = (place == spot - 1) | (place == spot + 1)
-
-            @pl.when(~near | (tilt < last))
-            def _():
-                send_side(block, tilt).wait_send()
-
-        return carry
-
-    @pl.when(can_up)
-    def _():
-        send_up(partner, last).wait_send()
-
-    @pl.when(can_down)
-    def _():
-        send_down(partner, last).wait_send()
-
     def settle_blk(step, carry):
         peer = lax.rem(blk + step, blocks)
         send_foot(peer).wait_send()
@@ -426,7 +427,6 @@
         part_copy(lax.rem(gy + step, groups), gy).wait_send()
         return carry
 
-    lax.fori_loop(0, line, settle_line, 0)
     lax.fori_loop(1, blocks, settle_blk, 0)
     lax.fori_loop(1, groups, settle_gy, 0)
 

time: 46.1 us -> 46 us (level)
  no operation moved by 1% of the time
where the time goes in v5:
time: 46 us; the launch traced here: 45.8 us
  Pallas kernels  45 us (98%)
  local copies, waits for them, and re-layouts  0.8 us (2%)
    pallas_call x1, Pallas kernels, per_device(): pl.pallas_call(functools.partial(kernel, blocks, groups), out_shape=pltpu...  45 us

profile of v5, /device:TPU:0, one launch (start us, length us, event | category | flops | bytes accessed | tf_op | source)
XLA Modules:
  0.0 45.8 jit_solution(4806729662780552077)
XLA Ops:
  0.0 45.0 %shard_map.64 = f32[256,512]{1,0:T(8,128)S(1)} custom-call(f32[256,512]{1,0:T(8,128)} %bitcast.5, f32[2,2816]{1,0:T(2,128)} %bitcast.6, f32[2,2816]{1,0:T(2,128)} %row_hbm.1, f32[256,512]{1,0:T(8,128)} %col_hbm.1, bf16[2,512,128]{2,1,0:T(8,128)(2,1)} %band_ref.1, s32[8,16]{1,0:T(8,128)} %bitcast.7), custom_call_target="tpu_custom_call" | custom-call | flops 1073741824 | bytes 1572864 | tf_op jit(solution)/shard_map/pallas_call | solution.py:442
  45.1 0.8 %copy.8 = f32[1,256,512]{2,1,0:T(8,128)} copy(f32[1,256,512]{2,1,0:T(8,128)S(1)} %bitcast.4) | data formatting | bytes 1048576
